TPU v7x, 1024 devices: a whole 4x4x32 slice. The times are simulated.
1024 devices in a mesh: tables: 64 (over z, core), cols: 16 (over y, x).
Axes of the slice: x: 4, y: 4, z: 32, core: 2. Of those that a mesh axis runs over, the one named last changes fastest.
Arguments:
- pooled_grad: bfloat16 [128, 1024, 8192], P(None, 'cols', 'tables'), may hold values from -6 to 6
- bag_ids: int32 [128, 8, 8192], P('tables'), may hold values from 0 to 1023
- bag_lengths: int32 [128, 8192], P('tables'), may hold values from 1 to 8
- table_rows: float32 [128, 1024, 1024], P('tables', 'cols'), may hold values from -6 to 6
- row_state: float32 [128, 1024], P('tables'), may hold values from 0.1 to 2
Outputs:
- new_rows: float32 [128, 1024, 1024], P('tables', 'cols')
- new_state: float32 [128, 1024], P('tables')
Inputs may be any that keep to these rules, and one draw needn't show every extreme that they name: `bag_lengths`: ids at positions at or past a bag's length are ignored.
All inputs are finite; a program needn't handle non-finite values.
Results may differ from a plain program's by a relative error of at most 0.0003.
Values may be sent and summed in bfloat16 or wider, within the bound.
No kernel may reach another device: no remote copies, remote signals or barrier semaphores. Data moves between devices by JAX's collectives and lax.ppermute only.
A program may use at most 32 MiB of HBM per device.

v0:
```python
import jax
import jax.numpy as jnp
from jax import lax
from jax.sharding import PartitionSpec as P

WIDTH = 1024


learning_rate = 0.1
epsilon = 1e-06


def table_gradient(arrived, row_ids, lengths_now, row_count, block_rows):
    columns = arrived.shape[0]
    targets = jnp.arange(row_count, dtype=jnp.int32)
    blocks = arrived.shape[1] // block_rows

    def one_block(number, total):
        start = number * block_rows
        ids_block = lax.dynamic_slice_in_dim(row_ids, start, block_rows, 1)
        lens_block = lax.dynamic_slice_in_dim(lengths_now, start, block_rows, 0)
        grads_block = lax.dynamic_slice_in_dim(arrived, start, block_rows, 1)
        counts = jnp.zeros((block_rows, row_count), jnp.float32)
        for place in range(ids_block.shape[0]):
            active = place < lens_block
            matches = (ids_block[place][:, None] == targets[None, :]) & active[:, None]
            counts = counts + matches.astype(jnp.float32)
        counts = counts.astype(jnp.bfloat16)
        return total + jnp.dot(grads_block, counts, preferred_element_type=jnp.float32)

    empty = jnp.zeros((columns, row_count), jnp.float32)
    return lax.fori_loop(0, blocks, one_block, empty)


def body(pooled_grad, bag_ids, bag_lengths, table_rows, row_state):
    group_size = table_rows.shape[0]
    row_count = table_rows.shape[2]
    columns = pooled_grad.shape[1]
    owners = pooled_grad.shape[2]
    groups = lax.axis_size("tables")
    shards_block = min(groups, max(1, 1024 // owners))
    block_rows = owners * shards_block
    slices = []
    grouped = pooled_grad.reshape(groups, group_size, columns, owners)
    for member in range(group_size):
        received = lax.all_to_all(
            grouped[:, member], "tables", split_axis=0, concat_axis=2, tiled=True
        )
        slices.append(received[0])
    gradients = []
    squares = []
    for member in range(group_size):
        gradient = table_gradient(
            slices[member], bag_ids[member], bag_lengths[member], row_count, block_rows
        )
        gradients.append(gradient)
        squares.append(lax.psum(jnp.sum(gradient * gradient, axis=0), "cols"))
    totals = jnp.stack(squares)
    stacked = jnp.stack(gradients)
    new_state = row_state + totals / WIDTH
    new_rows = table_rows - learning_rate * stacked / (jnp.sqrt(new_state)[:, None, :] + epsilon)
    return (new_rows, new_state)


def solution(mesh):
    placed = (
        P(None, "cols", "tables"),
        P("tables", None, None),
        P("tables", None),
        P("tables", "cols", None),
        P("tables", None),
    )
    return jax.shard_map(
        body,
        mesh=mesh,
        in_specs=placed,
        out_specs=(P("tables", "cols", None), P("tables", None)),
        check_vma=False,
    )
```

profile of v0, /device:TPU:32, one launch (start us, length us, event | category | flops | bytes accessed | tf_op | source)
XLA Modules:
  0.0 357.8 jit_solution(1083246918778802511)
XLA Ops:
  0.6 3.0 slice_bitcast_fusion.1
  3.7 0.0 copy-start.1
  3.7 29.1 %all-to-all-start = ((bf16[64,64,128]{2,1,0:T(8,128)(2,1)}), bf16[64,64,128]{2,1,0:T(8,128)(2,1)S(1)}, u32[]{:S(2)}, u32[]{:S(2)}) async-start(bf16[64,64,128]{2,1,0:T(8,128)(2,1)} %get-tuple-element.404), calls=%async_computation | async-start | bytes 2097152 | tf_op jit(solution)/shard_map/all_to_all | solution.py:46
  32.8 0.0 copy-done.1
  32.8 0.0 copy-start.2
  32.9 108.4 %all-to-all-done = bf16[64,64,128]{2,1,0:T(8,128)(2,1)S(1)} async-done(((bf16[64,64,128]{2,1,0:T(8,128)(2,1)}), bf16[64,64,128]{2,1,0:T(8,128)(2,1)S(1)}, u32[]{:S(2)}, u32[]{:S(2)}) %all-to-all-start) | async-done | bytes 1048608 | tf_op jit(solution)/shard_map/all_to_all | solution.py:46
  141.2 6.8 %all-to-all-start.1 = ((bf16[64,64,128]{2,1,0:T(8,128)(2,1)}), bf16[64,64,128]{2,1,0:T(8,128)(2,1)S(1)}, u32[]{:S(2)}, u32[]{:S(2)}) async-start(bf16[64,64,128]{2,1,0:T(8,128)(2,1)} %get-tuple-element.405), calls=%async_computation.1 | async-start | bytes 2097152 | tf_op jit(solution)/shard_map/all_to_all | solution.py:46
  148.1 0.0 copy-done.2
  148.1 0.1 fusion.48
  148.1 0.7 copy.9
  148.8 0.7 copy.16
  149.5 55.5 %while.30 = (s32[]{:T(128)}, f32[64,1024]{1,0:T(8,128)S(1)}, bf16[64,8192]{1,0:T(8,128)(2,1)S(1)}, s32[8,8192]{1,0:T(8,128)S(1)}, s32[8192]{0:T(1024)S(1)}, /*in...) while((s32[]{:T(128)}, f32[64,1024]{1,0:T(8,128)S(1)}, ...), condition=%wide.region_1.0_spmd.clone.clone, body=%wide.region_0.0_spmd.clone.clone.sunk | while | flops 167911440 | bytes 774473 | solution.py:32
  149.5 0.1 constant_dynamic-slice_fusion.4
  149.7 6.7 %fusion.54 = f32[64,1024]{1,0:T(8,128)S(1)} fusion(s32[1024]{0:T(1024)S(1)} %bitcast.95, s32[1024]{0:T(1024)S(1)} %bitcast.89, s32[1024]{0:T(1024)S(1)} %bitcast.90, s32[1024]{0:T(1024)S(1)} %bitcast.91, s32[1024]{0:T(1024)S(1)} %bitcast.92, s32[1024]{0:T(1024)S(1)} %bitcast.93, s32[1024]{0:T(1024)S(1)} %bitcast.94, s32[1024]{0:T(1024)S(1)} %bitcast.88, ...), kind=kOutput, calls=%fused_computation.28.clone.1 | convolution fusion | flops 167903232 | bytes 696325 | tf_op jit(solution)/shard_map/while/body/eval_jaxpr/dot_general | solution.py:29
  156.5 0.1 constant_dynamic-slice_fusion.4
  156.7 6.7 %fusion.54 = f32[64,1024]{1,0:T(8,128)S(1)} fusion(s32[1024]{0:T(1024)S(1)} %bitcast.95, s32[1024]{0:T(1024)S(1)} %bitcast.89, s32[1024]{0:T(1024)S(1)} %bitcast.90, s32[1024]{0:T(1024)S(1)} %bitcast.91, s32[1024]{0:T(1024)S(1)} %bitcast.92, s32[1024]{0:T(1024)S(1)} %bitcast.93, s32[1024]{0:T(1024)S(1)} %bitcast.94, s32[1024]{0:T(1024)S(1)} %bitcast.88, ...), kind=kOutput, calls=%fused_computation.28.clone.1 | convolution fusion | flops 167903232 | bytes 696325 | tf_op jit(solution)/shard_map/while/body/eval_jaxpr/dot_general | solution.py:29
  163.4 0.1 constant_dynamic-slice_fusion.4
  163.6 6.7 %fusion.54 = f32[64,1024]{1,0:T(8,128)S(1)} fusion(s32[1024]{0:T(1024)S(1)} %bitcast.95, s32[1024]{0:T(1024)S(1)} %bitcast.89, s32[1024]{0:T(1024)S(1)} %bitcast.90, s32[1024]{0:T(1024)S(1)} %bitcast.91, s32[1024]{0:T(1024)S(1)} %bitcast.92, s32[1024]{0:T(1024)S(1)} %bitcast.93, s32[1024]{0:T(1024)S(1)} %bitcast.94, s32[1024]{0:T(1024)S(1)} %bitcast.88, ...), kind=kOutput, calls=%fused_computation.28.clone.1 | convolution fusion | flops 167903232 | bytes 696325 | tf_op jit(solution)/shard_map/while/body/eval_jaxpr/dot_general | solution.py:29
  170.4 0.1 constant_dynamic-slice_fusion.4
  170.6 6.7 %fusion.54 = f32[64,1024]{1,0:T(8,128)S(1)} fusion(s32[1024]{0:T(1024)S(1)} %bitcast.95, s32[1024]{0:T(1024)S(1)} %bitcast.89, s32[1024]{0:T(1024)S(1)} %bitcast.90, s32[1024]{0:T(1024)S(1)} %bitcast.91, s32[1024]{0:T(1024)S(1)} %bitcast.92, s32[1024]{0:T(1024)S(1)} %bitcast.93, s32[1024]{0:T(1024)S(1)} %bitcast.94, s32[1024]{0:T(1024)S(1)} %bitcast.88, ...), kind=kOutput, calls=%fused_computation.28.clone.1 | convolution fusion | flops 167903232 | bytes 696325 | tf_op jit(solution)/shard_map/while/body/eval_jaxpr/dot_general | solution.py:29
  177.3 0.1 constant_dynamic-slice_fusion.4
  177.5 6.7 %fusion.54 = f32[64,1024]{1,0:T(8,128)S(1)} fusion(s32[1024]{0:T(1024)S(1)} %bitcast.95, s32[1024]{0:T(1024)S(1)} %bitcast.89, s32[1024]{0:T(1024)S(1)} %bitcast.90, s32[1024]{0:T(1024)S(1)} %bitcast.91, s32[1024]{0:T(1024)S(1)} %bitcast.92, s32[1024]{0:T(1024)S(1)} %bitcast.93, s32[1024]{0:T(1024)S(1)} %bitcast.94, s32[1024]{0:T(1024)S(1)} %bitcast.88, ...), kind=kOutput, calls=%fused_computation.28.clone.1 | convolution fusion | flops 167903232 | bytes 696325 | tf_op jit(solution)/shard_map/while/body/eval_jaxpr/dot_general | solution.py:29
  184.3 0.1 constant_dynamic-slice_fusion.4
  184.4 6.7 %fusion.54 = f32[64,1024]{1,0:T(8,128)S(1)} fusion(s32[1024]{0:T(1024)S(1)} %bitcast.95, s32[1024]{0:T(1024)S(1)} %bitcast.89, s32[1024]{0:T(1024)S(1)} %bitcast.90, s32[1024]{0:T(1024)S(1)} %bitcast.91, s32[1024]{0:T(1024)S(1)} %bitcast.92, s32[1024]{0:T(1024)S(1)} %bitcast.93, s32[1024]{0:T(1024)S(1)} %bitcast.94, s32[1024]{0:T(1024)S(1)} %bitcast.88, ...), kind=kOutput, calls=%fused_computation.28.clone.1 | convolution fusion | flops 167903232 | bytes 696325 | tf_op jit(solution)/shard_map/while/body/eval_jaxpr/dot_general | solution.py:29
  191.2 0.1 constant_dynamic-slice_fusion.4
  191.4 6.7 %fusion.54 = f32[64,1024]{1,0:T(8,128)S(1)} fusion(s32[1024]{0:T(1024)S(1)} %bitcast.95, s32[1024]{0:T(1024)S(1)} %bitcast.89, s32[1024]{0:T(1024)S(1)} %bitcast.90, s32[1024]{0:T(1024)S(1)} %bitcast.91, s32[1024]{0:T(1024)S(1)} %bitcast.92, s32[1024]{0:T(1024)S(1)} %bitcast.93, s32[1024]{0:T(1024)S(1)} %bitcast.94, s32[1024]{0:T(1024)S(1)} %bitcast.88, ...), kind=kOutput, calls=%fused_computation.28.clone.1 | convolution fusion | flops 167903232 | bytes 696325 | tf_op jit(solution)/shard_map/while/body/eval_jaxpr/dot_general | solution.py:29
  198.1 0.1 constant_dynamic-slice_fusion.4
  198.3 6.7 %fusion.54 = f32[64,1024]{1,0:T(8,128)S(1)} fusion(s32[1024]{0:T(1024)S(1)} %bitcast.95, s32[1024]{0:T(1024)S(1)} %bitcast.89, s32[1024]{0:T(1024)S(1)} %bitcast.90, s32[1024]{0:T(1024)S(1)} %bitcast.91, s32[1024]{0:T(1024)S(1)} %bitcast.92, s32[1024]{0:T(1024)S(1)} %bitcast.93, s32[1024]{0:T(1024)S(1)} %bitcast.94, s32[1024]{0:T(1024)S(1)} %bitcast.88, ...), kind=kOutput, calls=%fused_computation.28.clone.1 | convolution fusion | flops 167903232 | bytes 696325 | tf_op jit(solution)/shard_map/while/body/eval_jaxpr/dot_general | solution.py:29
  205.1 52.8 %all-to-all-done.1 = bf16[64,64,128]{2,1,0:T(8,128)(2,1)S(1)} async-done(((bf16[64,64,128]{2,1,0:T(8,128)(2,1)}), bf16[64,64,128]{2,1,0:T(8,128)(2,1)S(1)}, u32[]{:S(2)}, u32[]{:S(2)}) %all-to-all-start.1) | async-done | bytes 1048608 | tf_op jit(solution)/shard_map/all_to_all | solution.py:46
  257.9 0.7 copy.10
  258.6 0.7 copy.15
  259.3 0.0 copy-start.3
  259.3 0.0 copy-start
  259.3 55.7 %while.31 = (s32[]{:T(128)}, f32[64,1024]{1,0:T(8,128)S(1)}, bf16[64,8192]{1,0:T(8,128)(2,1)S(1)}, s32[8,8192]{1,0:T(8,128)S(1)}, s32[8192]{0:T(1024)S(1)}, /*in...) while((s32[]{:T(128)}, f32[64,1024]{1,0:T(8,128)S(1)}, ...), condition=%wide.region_3.0_spmd.clone.clone, body=%wide.region_2.0_spmd.clone.clone.sunk | while | flops 167911440 | bytes 774473 | solution.py:32
  259.5 0.1 constant_dynamic-slice_fusion.5
  259.7 6.7 %fusion.56 = f32[64,1024]{1,0:T(8,128)S(1)} fusion(s32[1024]{0:T(1024)S(1)} %bitcast.103, s32[1024]{0:T(1024)S(1)} %bitcast.97, s32[1024]{0:T(1024)S(1)} %bitcast.98, s32[1024]{0:T(1024)S(1)} %bitcast.99, s32[1024]{0:T(1024)S(1)} %bitcast.100, s32[1024]{0:T(1024)S(1)} %bitcast.101, s32[1024]{0:T(1024)S(1)} %bitcast.102, s32[1024]{0:T(1024)S(1)} %bitcast.96, ...), kind=kOutput, calls=%fused_computation.66.clone.1 | convolution fusion | flops 167903232 | bytes 696325 | tf_op jit(solution)/shard_map/while/body/eval_jaxpr/dot_general | solution.py:29
  266.4 0.1 constant_dynamic-slice_fusion.5
  266.6 6.7 %fusion.56 = f32[64,1024]{1,0:T(8,128)S(1)} fusion(s32[1024]{0:T(1024)S(1)} %bitcast.103, s32[1024]{0:T(1024)S(1)} %bitcast.97, s32[1024]{0:T(1024)S(1)} %bitcast.98, s32[1024]{0:T(1024)S(1)} %bitcast.99, s32[1024]{0:T(1024)S(1)} %bitcast.100, s32[1024]{0:T(1024)S(1)} %bitcast.101, s32[1024]{0:T(1024)S(1)} %bitcast.102, s32[1024]{0:T(1024)S(1)} %bitcast.96, ...), kind=kOutput, calls=%fused_computation.66.clone.1 | convolution fusion | flops 167903232 | bytes 696325 | tf_op jit(solution)/shard_map/while/body/eval_jaxpr/dot_general | solution.py:29
  273.4 0.1 constant_dynamic-slice_fusion.5
  273.6 6.7 %fusion.56 = f32[64,1024]{1,0:T(8,128)S(1)} fusion(s32[1024]{0:T(1024)S(1)} %bitcast.103, s32[1024]{0:T(1024)S(1)} %bitcast.97, s32[1024]{0:T(1024)S(1)} %bitcast.98, s32[1024]{0:T(1024)S(1)} %bitcast.99, s32[1024]{0:T(1024)S(1)} %bitcast.100, s32[1024]{0:T(1024)S(1)} %bitcast.101, s32[1024]{0:T(1024)S(1)} %bitcast.102, s32[1024]{0:T(1024)S(1)} %bitcast.96, ...), kind=kOutput, calls=%fused_computation.66.clone.1 | convolution fusion | flops 167903232 | bytes 696325 | tf_op jit(solution)/shard_map/while/body/eval_jaxpr/dot_general | solution.py:29
  280.3 0.1 constant_dynamic-slice_fusion.5
  280.5 6.7 %fusion.56 = f32[64,1024]{1,0:T(8,128)S(1)} fusion(s32[1024]{0:T(1024)S(1)} %bitcast.103, s32[1024]{0:T(1024)S(1)} %bitcast.97, s32[1024]{0:T(1024)S(1)} %bitcast.98, s32[1024]{0:T(1024)S(1)} %bitcast.99, s32[1024]{0:T(1024)S(1)} %bitcast.100, s32[1024]{0:T(1024)S(1)} %bitcast.101, s32[1024]{0:T(1024)S(1)} %bitcast.102, s32[1024]{0:T(1024)S(1)} %bitcast.96, ...), kind=kOutput, calls=%fused_computation.66.clone.1 | convolution fusion | flops 167903232 | bytes 696325 | tf_op jit(solution)/shard_map/while/body/eval_jaxpr/dot_general | solution.py:29
  287.3 0.1 constant_dynamic-slice_fusion.5
  287.4 6.7 %fusion.56 = f32[64,1024]{1,0:T(8,128)S(1)} fusion(s32[1024]{0:T(1024)S(1)} %bitcast.103, s32[1024]{0:T(1024)S(1)} %bitcast.97, s32[1024]{0:T(1024)S(1)} %bitcast.98, s32[1024]{0:T(1024)S(1)} %bitcast.99, s32[1024]{0:T(1024)S(1)} %bitcast.100, s32[1024]{0:T(1024)S(1)} %bitcast.101, s32[1024]{0:T(1024)S(1)} %bitcast.102, s32[1024]{0:T(1024)S(1)} %bitcast.96, ...), kind=kOutput, calls=%fused_computation.66.clone.1 | convolution fusion | flops 167903232 | bytes 696325 | tf_op jit(solution)/shard_map/while/body/eval_jaxpr/dot_general | solution.py:29
  294.2 0.1 constant_dynamic-slice_fusion.5
  294.4 6.7 %fusion.56 = f32[64,1024]{1,0:T(8,128)S(1)} fusion(s32[1024]{0:T(1024)S(1)} %bitcast.103, s32[1024]{0:T(1024)S(1)} %bitcast.97, s32[1024]{0:T(1024)S(1)} %bitcast.98, s32[1024]{0:T(1024)S(1)} %bitcast.99, s32[1024]{0:T(1024)S(1)} %bitcast.100, s32[1024]{0:T(1024)S(1)} %bitcast.101, s32[1024]{0:T(1024)S(1)} %bitcast.102, s32[1024]{0:T(1024)S(1)} %bitcast.96, ...), kind=kOutput, calls=%fused_computation.66.clone.1 | convolution fusion | flops 167903232 | bytes 696325 | tf_op jit(solution)/shard_map/while/body/eval_jaxpr/dot_general | solution.py:29
  301.1 0.1 constant_dynamic-slice_fusion.5
  301.3 6.7 %fusion.56 = f32[64,1024]{1,0:T(8,128)S(1)} fusion(s32[1024]{0:T(1024)S(1)} %bitcast.103, s32[1024]{0:T(1024)S(1)} %bitcast.97, s32[1024]{0:T(1024)S(1)} %bitcast.98, s32[1024]{0:T(1024)S(1)} %bitcast.99, s32[1024]{0:T(1024)S(1)} %bitcast.100, s32[1024]{0:T(1024)S(1)} %bitcast.101, s32[1024]{0:T(1024)S(1)} %bitcast.102, s32[1024]{0:T(1024)S(1)} %bitcast.96, ...), kind=kOutput, calls=%fused_computation.66.clone.1 | convolution fusion | flops 167903232 | bytes 696325 | tf_op jit(solution)/shard_map/while/body/eval_jaxpr/dot_general | solution.py:29
  308.1 0.1 constant_dynamic-slice_fusion.5
  308.3 6.7 %fusion.56 = f32[64,1024]{1,0:T(8,128)S(1)} fusion(s32[1024]{0:T(1024)S(1)} %bitcast.103, s32[1024]{0:T(1024)S(1)} %bitcast.97, s32[1024]{0:T(1024)S(1)} %bitcast.98, s32[1024]{0:T(1024)S(1)} %bitcast.99, s32[1024]{0:T(1024)S(1)} %bitcast.100, s32[1024]{0:T(1024)S(1)} %bitcast.101, s32[1024]{0:T(1024)S(1)} %bitcast.102, s32[1024]{0:T(1024)S(1)} %bitcast.96, ...), kind=kOutput, calls=%fused_computation.66.clone.1 | convolution fusion | flops 167903232 | bytes 696325 | tf_op jit(solution)/shard_map/while/body/eval_jaxpr/dot_general | solution.py:29
  315.1 41.2 %all-reduce = (f32[1,1024]{1,0:T(1,128)S(1)}, f32[1,1024]{1,0:T(1,128)S(1)}) all-reduce(f32[1,1024]{1,0:T(1,128)S(1)} %bitcast.107, f32[1,1024]{1,0:T(1,128)S(1)} %bitcast.106), channel_id=1, replica_groups=mesh['tables'=64,'cols'=16] {'cols'}, use_global_device_ids=true, to_apply=%region_7.0 | all-reduce | flops 2048 | bytes 16384 | tf_op jit(solution)/shard_map/psum | solution.py:57
  356.2 0.0 copy-done.3
  356.3 0.6 sqrt_add_fusion
  356.9 0.0 copy-done
  356.9 0.9 fusion.45
  (21 shorter events, 0.4 us)
Async XLA Ops:
  3.7 29.1 %copy-start.1 = (s32[2,8,8192]{2,1,0:T(8,128)S(1)}, s32[2,8,8192]{2,1,0:T(8,128)}, u32[]{:S(2)}) copy-start(s32[2,8,8192]{2,1,0:T(8,128)} %param.10) | copy-start | bytes 1572868
  3.7 137.6 %all-to-all-start = ((bf16[64,64,128]{2,1,0:T(8,128)(2,1)}), bf16[64,64,128]{2,1,0:T(8,128)(2,1)S(1)}, u32[]{:S(2)}, u32[]{:S(2)}) async-start(bf16[64,64,128]{2,1,0:T(8,128)(2,1)} %get-tuple-element.404), calls=%async_computation | async-start | bytes 2097152 | tf_op jit(solution)/shard_map/all_to_all | solution.py:46
  32.8 115.2 %copy-start.2 = (s32[2,8192]{1,0:T(2,128)S(1)}, s32[2,8192]{1,0:T(2,128)}, u32[]{:S(2)}) copy-start(s32[2,8192]{1,0:T(2,128)} %param.11) | copy-start | bytes 196612
  141.2 116.7 %all-to-all-start.1 = ((bf16[64,64,128]{2,1,0:T(8,128)(2,1)}), bf16[64,64,128]{2,1,0:T(8,128)(2,1)S(1)}, u32[]{:S(2)}, u32[]{:S(2)}) async-start(bf16[64,64,128]{2,1,0:T(8,128)(2,1)} %get-tuple-element.405), calls=%async_computation.1 | async-start | bytes 2097152 | tf_op jit(solution)/shard_map/all_to_all | solution.py:46
  259.3 97.0 %copy-start.3 = (f32[2,1024]{1,0:T(2,128)S(1)}, f32[2,1024]{1,0:T(2,128)}, u32[]{:S(2)}) copy-start(f32[2,1024]{1,0:T(2,128)} %param.13) | copy-start | bytes 24580
  259.3 97.6 %copy-start = (f32[2,64,1024]{2,1,0:T(8,128)S(1)}, f32[2,64,1024]{2,1,0:T(8,128)}, u32[]{:S(2)}) copy-start(f32[2,64,1024]{2,1,0:T(8,128)} %param.12) | copy-start | bytes 1572868
where the time goes:
time: 358 us
  waiting for transfers between devices  161 us (45%)
  matrix products  108 us (30%)
  blocking collectives  41.2 us (12%)
  starting transfers between devices  36 us (10%)
  local copies, waits for them, and re-layouts  8.26 us (2%)
    all_to_all x2, waiting for transfers between devices, body(): lax.all_to_all(grouped[:, member], 'tables', split_axis=0, concat_axis=2,...  161 us
    dot_general x16, matrix products, one_block(): jnp.dot(grads_block, counts, preferred_element_type=jnp.float32)  108 us
    psum x1, blocking collectives, body(): squares.append(lax.psum(jnp.sum(gradient * gradient, axis=0), 'cols'))  41.2 us
    all_to_all x2, starting transfers between devices, body(): lax.all_to_all(grouped[:, member], 'tables', split_axis=0, concat_axis=2,...  36 us
  transfers between devices with their start and end apart: 2, of which 2 were waited for; matrix products, arithmetic and copies ran while one was open for 16% of the time, Pallas kernels for 0%

commit v1 on v0

v1 whole, which is shorter than its diff:
```python
import jax
import jax.numpy as jnp
from jax import lax
from jax.experimental import pallas as pl
from jax.experimental.pallas import tpu as pltpu
from jax.sharding import PartitionSpec as P

WIDTH = 1024
learning_rate = 0.1
epsilon = 1e-06

LOW = 128
DIGITS = 8


def words_kernel(ids_ref, lens_ref, words_ref):
    table = pl.program_id(0)
    ids = ids_ref[0]
    lens = lens_ref[pl.ds(table, 1), :]
    samples = ids.shape[1]
    word = lax.broadcasted_iota(jnp.int32, (LOW, samples), 0)
    place = lax.broadcasted_iota(jnp.int32, ids.shape, 0)
    unit = jnp.where(place < lens, lax.shift_left(jnp.int32(1), (ids >> 7) * 4), 0)
    low = ids & (LOW - 1)
    total = jnp.zeros((LOW, samples), jnp.int32)
    for position in range(ids.shape[0]):
        total = total + jnp.where(
            low[position : position + 1] == word, unit[position : position + 1], 0
        )
    words_ref[0] = total


def count_words(ids, lens, block=2048):
    tables, places, samples = ids.shape
    return pl.pallas_call(
        words_kernel,
        grid=(tables, samples // block),
        in_specs=[
            pl.BlockSpec((1, places, block), lambda t, i: (t, 0, i)),
            pl.BlockSpec((tables, block), lambda t, i: (0, i)),
        ],
        out_specs=pl.BlockSpec((1, LOW, block), lambda t, i: (t, 0, i)),
        out_shape=jax.ShapeDtypeStruct((tables, LOW, samples), jnp.int32),
        cost_estimate=pl.CostEstimate(
            flops=40_000_000, bytes_accessed=8_000_000, transcendentals=0
        ),
        name="count_words",
    )(ids, lens)


def gradient_kernel(arrived_ref, words_ref, grad_ref, square_ref):
    step = pl.program_id(1)

    @pl.when(step == 0)
    def _():
        grad_ref[...] = jnp.zeros_like(grad_ref)

    grads = jnp.concatenate(
        [arrived_ref[j, 0] for j in range(arrived_ref.shape[0])], axis=1
    )
    words = words_ref[0]
    for digit in range(DIGITS):
        counts = lax.shift_right_logical(words, 4 * digit) & 15
        counts = counts.astype(jnp.float32).astype(jnp.bfloat16)
        grad_ref[0, :, LOW * digit : LOW * (digit + 1)] += lax.dot_general(
            grads, counts, (((1,), (1,)), ((), ())), preferred_element_type=jnp.float32
        )

    @pl.when(step == pl.num_programs(1) - 1)
    def _():
        grad = grad_ref[0]
        square_ref[0] = jnp.sum(grad * grad, axis=0, keepdims=True)


def gradients(arrived, words, block=16):
    sources, tables, columns, owned = arrived.shape
    rows = LOW * DIGITS
    return pl.pallas_call(
        gradient_kernel,
        grid=(tables, sources // block),
        in_specs=[
            pl.BlockSpec((block, 1, columns, owned), lambda t, i: (i, t, 0, 0)),
            pl.BlockSpec((1, LOW, owned * block), lambda t, i: (t, 0, i)),
        ],
        out_specs=[
            pl.BlockSpec((1, columns, rows), lambda t, i: (t, 0, 0)),
            pl.BlockSpec((1, 1, rows), lambda t, i: (t, 0, 0)),
        ],
        out_shape=[
            jax.ShapeDtypeStruct((tables, columns, rows), jnp.float32),
            jax.ShapeDtypeStruct((tables, 1, rows), jnp.float32),
        ],
        cost_estimate=pl.CostEstimate(
            flops=2_147_483_648, bytes_accessed=12_000_000, transcendentals=0
        ),
        name="gradients",
    )(arrived, words)


def body(pooled_grad, bag_ids, bag_lengths, table_rows, row_state):
    members, _, row_count = table_rows.shape
    columns, owned = pooled_grad.shape[1:]
    groups = lax.axis_size("tables")
    splits = lax.axis_size("cols")
    grouped = pooled_grad.reshape(groups, members, columns, owned)
    arrived = lax.all_to_all(grouped, "tables", 0, 0, tiled=True)
    words = count_words(bag_ids, bag_lengths)
    gradient, squares = gradients(arrived, words)
    squares = squares.reshape(members, row_count)
    shared = jnp.broadcast_to(squares[None], (splits, members, row_count))
    totals = jnp.sum(lax.all_to_all(shared, "cols", 0, 0, tiled=True), axis=0)
    new_state = row_state + totals / WIDTH
    new_rows = table_rows - learning_rate * gradient / (
        jnp.sqrt(new_state)[:, None, :] + epsilon
    )
    return (new_rows, new_state)


def solution(mesh):
    placed = (
        P(None, "cols", "tables"),
        P("tables", None, None),
        P("tables", None),
        P("tables", "cols", None),
        P("tables", None),
    )
    return jax.shard_map(
        body,
        mesh=mesh,
        in_specs=placed,
        out_specs=(P("tables", "cols", None), P("tables", None)),
        check_vma=False,
    )
```

time: 358 us -> 265 us (0.74)
  the two profiles are of different devices: /device:TPU:32 before, /device:TPU:2 now
where the time goes in v1:
time: 265 us; the launch traced here: 264 us
  waiting for transfers between devices  190 us (72%)
  starting transfers between devices  29.4 us (11%)
  Pallas kernels  26 us (10%)
  blocking collectives  13.9 us (5%)
    all_to_all x1, waiting for transfers between devices, body(): arrived = lax.all_to_all(grouped, 'tables', 0, 0, tiled=True)  190 us
    all_to_all x1, starting transfers between devices, body(): arrived = lax.all_to_all(grouped, 'tables', 0, 0, tiled=True)  29.4 us
    pallas_call x1, Pallas kernels, gradients(): pl.pallas_call(gradient_kernel, grid=(tables, sources // block), in_specs...  15 us
    all_to_all x1, blocking collectives, body(): totals = jnp.sum(lax.all_to_all(shared, 'cols', 0, 0, tiled=True), axis=0)  13.9 us
    pallas_call x1, Pallas kernels, count_words(): pl.pallas_call(words_kernel, grid=(tables, samples // block), in_specs=[p...  11 us
  transfers between devices with their start and end apart: 1, of which 1 were waited for; matrix products, arithmetic and copies ran while one was open for 0% of the time, Pallas kernels for 4%

profile of v1, /device:TPU:2, one launch (start us, length us, event | category | flops | bytes accessed | tf_op | source)
XLA Modules:
  0.0 264.1 jit_solution(2094989409422502316)
XLA Ops:
  0.6 29.4 %all-to-all-start = ((bf16[64,2,64,128]{3,2,1,0:T(8,128)(2,1)}), bf16[64,2,64,128]{3,2,1,0:T(8,128)(2,1)S(1)}, u32[]{:S(2)}, u32[]{:S(2)}) async-start(bf16[64,2,64,128]{3,2,1,0:T(8,128)(2,1)} %bitcast.4), calls=%async_computation | async-start | bytes 4194304 | tf_op jit(solution)/shard_map/all_to_all | solution.py:106
  30.0 11.0 %count_words.1.words_ref = s32[2,128,8192]{2,1,0:T(8,128)} custom-call(s32[2,8,8192]{2,1,0:T(8,128)} %ids_ref.1, s32[2,8192]{1,0:T(2,128)} %lens_ref.1), custom_call_target="tpu_custom_call" | custom-call | flops 40000000 | bytes 8000000 | tf_op jit(solution)/shard_map/count_words/pallas_call | solution.py:35
  41.0 0.0 copy-start.2
  41.0 0.0 copy-start.1
  41.0 189.5 %all-to-all-done.arrived_ref = bf16[64,2,64,128]{3,2,1,0:T(8,128)(2,1)S(1)} async-done(((bf16[64,2,64,128]{3,2,1,0:T(8,128)(2,1)}), bf16[64,2,64,128]{3,2,1,0:T(8,128)(2,1)S(1)}, u32[]{:S(2)}, u32[]{:S(2)}) %all-to-all-start) | async-done | bytes 2097184 | tf_op jit(solution)/shard_map/all_to_all | solution.py:106
  230.6 0.0 copy-start
  230.6 1.3 copy-done
  231.9 15.0 %gradients.1 = (f32[2,64,1024]{2,1,0:T(8,128)}, f32[2,1,1024]{2,1,0:T(1,128)}) custom-call(bf16[64,2,64,128]{3,2,1,0:T(8,128)(2,1)} %copy-done, s32[2,128,8192]{2,1,0:T(8,128)} %count_words.1.words_ref), custom_call_target="tpu_custom_call" | custom-call | flops 2147483648 | bytes 12000000 | tf_op jit(solution)/shard_map/gradients/pallas_call | solution.py:78
  246.9 0.7 copy.11
  247.6 13.9 %all_to_all.10 = f32[16,2,1024]{2,1,0:T(2,128)S(1)} all-to-all(f32[16,2,1024]{2,1,0:T(2,128)S(1)} %broadcast_in_dim.9), channel_id=1, replica_groups=mesh['tables'=64,'cols'=16] {'cols'}, dimensions={0} | all-to-all | bytes 262144 | tf_op jit(solution)/shard_map/all_to_all | solution.py:111
  261.5 0.1 reduce_sum.9
  261.6 0.0 copy-done.2
  261.6 0.6 sqrt_add_fusion
  262.2 0.0 copy-done.1
  262.2 1.9 divide_subtract_fusion
  (1 shorter events, 0.0 us)
Async XLA Ops:
  0.6 230.0 %all-to-all-start = ((bf16[64,2,64,128]{3,2,1,0:T(8,128)(2,1)}), bf16[64,2,64,128]{3,2,1,0:T(8,128)(2,1)S(1)}, u32[]{:S(2)}, u32[]{:S(2)}) async-start(bf16[64,2,64,128]{3,2,1,0:T(8,128)(2,1)} %bitcast.4), calls=%async_computation | async-start | bytes 4194304 | tf_op jit(solution)/shard_map/all_to_all | solution.py:106
  41.0 220.6 %copy-start.2 = (f32[2,1024]{1,0:T(2,128)S(1)}, f32[2,1024]{1,0:T(2,128)}, u32[]{:S(2)}) copy-start(f32[2,1024]{1,0:T(2,128)} %param.9) | copy-start | bytes 24580
  41.0 221.2 %copy-start.1 = (f32[2,64,1024]{2,1,0:T(8,128)S(1)}, f32[2,64,1024]{2,1,0:T(8,128)}, u32[]{:S(2)}) copy-start(f32[2,64,1024]{2,1,0:T(8,128)} %param.8) | copy-start | bytes 1572868
  230.6 1.4 copy-start

commit v2 on v0

v2 whole, which is shorter than its diff:
```python
import functools

import jax
import jax.numpy as jnp
from jax import lax
from jax.experimental import pallas as pl
from jax.experimental.pallas import tpu as pltpu
from jax.sharding import PartitionSpec as P

WIDTH = 1024
learning_rate = 0.1
epsilon = 1e-06

LOW = 128
DIGITS = 8
STRIDE = 15


def chip_at(place, core, chips):
    return (STRIDE * (place + core * (chips - 1 - 2 * place))) % chips


def place_of(chip, core, chips):
    place = (pow(STRIDE, -1, chips) * chip) % chips
    return place + core * (chips - 1 - 2 * place)


def pack_kernel(core_ref, grads_ref, packed_ref, held, in_done, out_done):
    chips = grads_ref.shape[0]
    reads = in_done.shape[0]
    size = chips // reads
    core = core_ref[0]

    def read(i):
        part = pl.ds(i * size, size)
        return pltpu.make_async_copy(grads_ref.at[part], held.at[part], in_done.at[i])

    def write(chip):
        place = place_of(chip, core, chips)
        return pltpu.make_async_copy(
            held.at[chip], packed_ref.at[place], out_done.at[chip]
        )

    for i in range(reads):
        read(i).start()
    for i in range(reads):
        read(i).wait()
        for chip in range(i * size, (i + 1) * size):
            write(chip).start()
    for chip in range(chips):
        write(chip).wait()


def pack(core, grads):
    return pl.pallas_call(
        pack_kernel,
        in_specs=[
            pl.BlockSpec(memory_space=pltpu.SMEM),
            pl.BlockSpec(memory_space=pl.ANY),
        ],
        out_specs=pl.BlockSpec(memory_space=pl.ANY),
        out_shape=jax.ShapeDtypeStruct(grads.shape, grads.dtype),
        scratch_shapes=[
            pltpu.VMEM(grads.shape, grads.dtype),
            pltpu.SemaphoreType.DMA((4,)),
            pltpu.SemaphoreType.DMA((grads.shape[0],)),
        ],
        cost_estimate=pl.CostEstimate(
            flops=0, bytes_accessed=4 * grads.size, transcendentals=0
        ),
        name="pack",
    )(core, grads)


def words_kernel(chips, owned, table, half, core_ref, ids_ref, lens_ref, words_ref):
    block = pl.program_id(0)
    source_core = core_ref[0] if half == 0 else 1 - core_ref[0]
    places = words_ref.shape[0] // owned
    word = lax.broadcasted_iota(jnp.int32, (LOW, owned), 0)
    for i in range(places):
        chip = chip_at(block * places + i, source_core, chips)
        start = pl.multiple_of((2 * chip + source_core) * owned, owned)
        ids = ids_ref[0, :, pl.ds(start, owned)]
        lens = lens_ref[:, pl.ds(start, owned)][table : table + 1]
        position = lax.broadcasted_iota(jnp.int32, ids.shape, 0)
        unit = jnp.where(
            position < lens, lax.shift_left(jnp.int32(1), (ids >> 7) * 4), 0
        )
        low = ids & (LOW - 1)
        total = jnp.zeros((LOW, owned), jnp.int32)
        for k in range(ids.shape[0]):
            total = total + jnp.where(low[k : k + 1] == word, unit[k : k + 1], 0)
        words_ref[owned * i : owned * (i + 1), :] = total.T


def count_words(core, ids, lens, chips, owned, table, half, block=8):
    tables, positions, samples = ids.shape
    return pl.pallas_call(
        functools.partial(words_kernel, chips, owned, table, half),
        grid=(chips // block,),
        in_specs=[
            pl.BlockSpec(memory_space=pltpu.SMEM),
            pl.BlockSpec((1, positions, samples), lambda i: (table, 0, 0)),
            pl.BlockSpec((tables, samples), lambda i: (0, 0)),
        ],
        out_specs=pl.BlockSpec((block * owned, LOW), lambda i: (i, 0)),
        out_shape=jax.ShapeDtypeStruct((chips * owned, LOW), jnp.int32),
        cost_estimate=pl.CostEstimate(
            flops=15_000_000, bytes_accessed=2_500_000, transcendentals=0
        ),
        name=f"count_words_{table}_{half}",
    )(core, ids, lens)


def multiply(arrived, words):
    grads = jnp.concatenate([arrived[j] for j in range(arrived.shape[0])], axis=1)
    products = []
    for pair in range(DIGITS // 2):
        counts, scales = [], []
        for digit in (2 * pair, 2 * pair + 1):
            top = digit == DIGITS - 1
            if top:
                held = lax.shift_right_logical(words, 4 * digit)
            else:
                held = words & (15 << (4 * digit))
            counts.append(held.astype(jnp.float32).astype(jnp.bfloat16))
            scales.append(1.0 if top else 16.0**-digit)
        product = jnp.dot(
            grads, jnp.concatenate(counts, axis=1), preferred_element_type=jnp.float32
        )
        lane = lax.broadcasted_iota(jnp.int32, product.shape, 1)
        products.append(product * jnp.where(lane < LOW, scales[0], scales[1]))
    return products


def part(pair):
    return slice(2 * LOW * pair, 2 * LOW * (pair + 1))


def own_kernel(table, core_ref, arrived_ref, words_ref, grad_ref):
    core = core_ref[0]
    arrived = [arrived_ref[j, core, table] for j in range(arrived_ref.shape[0])]
    for pair, product in enumerate(multiply(jnp.stack(arrived), words_ref[...])):
        grad_ref[:, part(pair)] = product


def own_half(core, arrived, words, table):
    columns = arrived.shape[3]
    return pl.pallas_call(
        functools.partial(own_kernel, table),
        in_specs=[
            pl.BlockSpec(memory_space=pltpu.SMEM),
            pl.BlockSpec(memory_space=pltpu.VMEM),
            pl.BlockSpec(memory_space=pltpu.VMEM),
        ],
        out_specs=pl.BlockSpec(memory_space=pltpu.VMEM),
        out_shape=jax.ShapeDtypeStruct((columns, LOW * DIGITS), jnp.float32),
        cost_estimate=pl.CostEstimate(
            flops=536_870_912, bytes_accessed=3_000_000, transcendentals=0
        ),
        compiler_params=pltpu.CompilerParams(vmem_limit_bytes=24 << 20),
        name=f"own_half_{table}",
    )(core, arrived, words)


def sibling_kernel(tables, *refs):
    arrived_ref = refs[0]
    words_refs, first_refs = refs[1 : 1 + tables], refs[1 + tables : 1 + 2 * tables]
    grad_ref, square_ref = refs[1 + 2 * tables :]
    for table in range(tables):
        products = multiply(arrived_ref[:, table], words_refs[table][...])
        for pair, product in enumerate(products):
            product = product + first_refs[table][:, part(pair)]
            grad_ref[table, :, part(pair)] = product
            square = jnp.sum(product * product, axis=0, keepdims=True)
            for copy in range(square_ref.shape[0]):
                square_ref[copy, table : table + 1, part(pair)] = square


def sibling_half(arrived, words, first, copies):
    _, tables, columns, _ = arrived.shape
    rows = LOW * DIGITS
    return pl.pallas_call(
        functools.partial(sibling_kernel, tables),
        in_specs=[pl.BlockSpec(memory_space=pltpu.VMEM)] * (1 + 2 * tables),
        out_specs=[pl.BlockSpec(memory_space=pltpu.VMEM)] * 2,
        out_shape=[
            jax.ShapeDtypeStruct((tables, columns, rows), jnp.float32),
            jax.ShapeDtypeStruct((copies, tables, rows), jnp.float32),
        ],
        cost_estimate=pl.CostEstimate(
            flops=1_073_741_824, bytes_accessed=6_000_000, transcendentals=0
        ),
        compiler_params=pltpu.CompilerParams(vmem_limit_bytes=24 << 20),
        name="sibling_half",
    )(arrived, *words, *first)


def body(pooled_grad, bag_ids, bag_lengths, table_rows, row_state):
    members = table_rows.shape[0]
    columns, owned = pooled_grad.shape[1:]
    groups = lax.axis_size("tables")
    splits = lax.axis_size("cols")
    chips = groups // 2
    core = (lax.axis_index("tables") % 2).astype(jnp.int32).reshape(1)
    orders = [
        [2 * chip_at(place, c, chips) + c for place in range(chips)] for c in range(2)
    ]
    grouped = pooled_grad.reshape(chips, 2, members, columns, owned)
    arrived = lax.all_to_all(
        pack(core, grouped), "tables", 0, 0, tiled=True, axis_index_groups=orders
    )
    words = [
        [
            count_words(core, bag_ids, bag_lengths, chips, owned, table, half)
            for table in range(members)
        ]
        for half in range(2)
    ]
    arrived, words = lax.optimization_barrier((arrived, words))
    other = lax.dynamic_index_in_dim(arrived, 1 - core[0], 1, keepdims=False)
    swapped = lax.ppermute(other, "tables", [(k, k ^ 1) for k in range(groups)])
    first = [own_half(core, arrived, words[0][table], table) for table in range(members)]
    gradient, squares = sibling_half(swapped, words[1], first, splits)
    totals = jnp.sum(lax.all_to_all(squares, "cols", 0, 0, tiled=True), axis=0)
    new_state = row_state + totals / WIDTH
    scale = learning_rate / (jnp.sqrt(new_state) + epsilon)
    new_rows = table_rows - scale[:, None, :] * gradient
    return (new_rows, new_state)


def solution(mesh):
    placed = (
        P(None, "cols", "tables"),
        P("tables", None, None),
        P("tables", None),
        P("tables", "cols", None),
        P("tables", None),
    )
    return jax.shard_map(
        body,
        mesh=mesh,
        in_specs=placed,
        out_specs=(P("tables", "cols", None), P("tables", None)),
        check_vma=False,
    )
```

time: 358 us -> 242 us (0.68)
  the two profiles are of different devices: /device:TPU:32 before, /device:TPU:128 now
where the time goes in v2:
time: 242 us
  waiting for transfers between devices  168 us (69%)
  starting transfers between devices  29.5 us (12%)
  Pallas kernels  26.7 us (11%)
  blocking collectives  14.8 us (6%)
    all_to_all x1, waiting for transfers between devices, body(): lax.all_to_all(pack(core, grouped), 'tables', 0, 0, tiled=True, axis_inde...  168 us
    all_to_all x1, starting transfers between devices, body(): lax.all_to_all(pack(core, grouped), 'tables', 0, 0, tiled=True, axis_inde...  27.3 us
    pallas_call x4, Pallas kernels, count_words(): pl.pallas_call(functools.partial(words_kernel, chips, owned, table, half)...  16.6 us
    all_to_all x1, blocking collectives, body(): totals = jnp.sum(lax.all_to_all(squares, 'cols', 0, 0, tiled=True), axis=0)  14.8 us
  transfers between devices with their start and end apart: 2, of which 1 were waited for; matrix products, arithmetic and copies ran while one was open for 0% of the time, Pallas kernels for 8%

profile of v2, /device:TPU:128, one launch (start us, length us, event | category | flops | bytes accessed | tf_op | source)
XLA Modules:
  0.0 242.1 jit_solution(2276611567489272719)
XLA Ops:
  0.6 2.7 %pack.1 = bf16[32,2,2,64,128]{4,3,2,1,0:T(8,128)(2,1)} custom-call(s32[1]{0:T(128)} %bitcast.core_ref, bf16[32,2,2,64,128]{4,3,2,1,0:T(8,128)(2,1)} %bitcast.4), custom_call_target="tpu_custom_call" | custom-call | bytes 4194304 | tf_op jit(solution)/shard_map/pack/pallas_call | solution.py:55
  3.3 27.3 %all-to-all-start = ((bf16[32,2,2,64,128]{4,3,2,1,0:T(8,128)(2,1)}), bf16[32,2,2,64,128]{4,3,2,1,0:T(8,128)(2,1)S(1)}, u32[]{:S(2)}, u32[]{:S(2)}) async-start(bf16[32,2,2,64,128]{4,3,2,1,0:T(8,128)(2,1)} %pack.1), calls=%async_computation | async-start | bytes 4194304 | tf_op jit(solution)/shard_map/all_to_all | solution.py:210
  30.7 4.2 %count_words_0_0.1.words_ref = s32[4096,128]{1,0:T(8,128)} custom-call(s32[1]{0:T(128)} %bitcast.core_ref, s32[2,8,8192]{2,1,0:T(8,128)} %ids_ref.7, s32[2,8192]{1,0:T(2,128)} %lens_ref.7), custom_call_target="tpu_custom_call" | custom-call | flops 15000000 | bytes 2500000 | tf_op jit(solution)/shard_map/count_words_0_0/pallas_call | solution.py:98
  34.8 4.2 %count_words_1_0.1.words_ref = s32[4096,128]{1,0:T(8,128)} custom-call(s32[1]{0:T(128)} %bitcast.core_ref, s32[2,8,8192]{2,1,0:T(8,128)} %ids_ref.7, s32[2,8192]{1,0:T(2,128)} %lens_ref.7), custom_call_target="tpu_custom_call" | custom-call | flops 15000000 | bytes 2500000 | tf_op jit(solution)/shard_map/count_words_1_0/pallas_call | solution.py:98
  39.0 4.1 %count_words_0_1.1.refs_1_ = s32[4096,128]{1,0:T(8,128)} custom-call(s32[1]{0:T(128)} %bitcast.core_ref, s32[2,8,8192]{2,1,0:T(8,128)} %ids_ref.7, s32[2,8192]{1,0:T(2,128)} %lens_ref.7), custom_call_target="tpu_custom_call" | custom-call | flops 15000000 | bytes 2500000 | tf_op jit(solution)/shard_map/count_words_0_1/pallas_call | solution.py:98
  43.1 4.2 %count_words_1_1.1.refs_2_ = s32[4096,128]{1,0:T(8,128)} custom-call(s32[1]{0:T(128)} %bitcast.core_ref, s32[2,8,8192]{2,1,0:T(8,128)} %ids_ref.7, s32[2,8192]{1,0:T(2,128)} %lens_ref.7), custom_call_target="tpu_custom_call" | custom-call | flops 15000000 | bytes 2500000 | tf_op jit(solution)/shard_map/count_words_1_1/pallas_call | solution.py:98
  47.3 168.3 %all-to-all-done.arrived_ref = bf16[32,2,2,64,128]{4,3,2,1,0:T(8,128)(2,1)S(1)} async-done(((bf16[32,2,2,64,128]{4,3,2,1,0:T(8,128)(2,1)}), bf16[32,2,2,64,128]{4,3,2,1,0:T(8,128)(2,1)S(1)}, u32[]{:S(2)}, u32[]{:S(2)}) %all-to-all-start) | async-done | bytes 2097184 | tf_op jit(solution)/shard_map/all_to_all | solution.py:210
  215.6 0.0 copy-start.1
  215.6 0.1 dynamic-slice_bitcast_fusion
  215.7 0.0 copy-start
  215.7 2.2 collective-permute-start
  217.9 0.0 copy-done.1
  217.9 1.9 own_half_1.1.refs_4_
  219.8 0.0 copy-done
  219.8 0.0 copy-start.2
  219.8 0.0 copy-start.3
  219.8 1.9 own_half_0.1.refs_3_
  221.7 0.0 copy-start.5
  221.7 0.0 copy-start.4
  221.7 0.0 collective-permute-done.refs_0_
  221.7 0.0 copy-done.2
  221.7 0.3 copy-done.3
  222.0 3.7 %sibling_half.1 = (f32[2,64,1024]{2,1,0:T(8,128)S(1)}, f32[16,2,1024]{2,1,0:T(2,128)S(1)}) custom-call(bf16[32,2,64,128]{3,2,1,0:T(8,128)(2,1)S(1)} %collective-permute-done.refs_0_, s32[4096,128]{1,0:T(8,128)S(1)} %copy-done.2, s32[4096,128]{1,0:T(8,128)S(1)} %copy-done.3, f32[64,1024]{1,0:T(8,128)S(1)} %own_half_0.1.refs_3_, f32[64,1024]{1,0:T(8,128)S(1)} %own_half_1.1.refs_4_), custom_call_target="tpu_custom_call" | custom-call | flops 1073741824 | bytes 6000000 | tf_op jit(solution)/shard_map/sibling_half/pallas_call | solution.py:183
  225.7 14.8 %all_to_all.10 = f32[16,2,1024]{2,1,0:T(2,128)S(1)} all-to-all(f32[16,2,1024]{2,1,0:T(2,128)S(1)} %get-tuple-element.14), channel_id=1, replica_groups=mesh['tables'=64,'cols'=16] {'cols'}, dimensions={0} | all-to-all | bytes 262144 | tf_op jit(solution)/shard_map/all_to_all | solution.py:225
  240.5 0.1 reduce_sum.9
  240.6 0.0 copy-done.5
  240.6 0.6 add_divide_fusion
  241.2 0.0 copy-done.4
  241.2 0.9 multiply_subtract_fusion
Async XLA Ops:
  3.3 212.3 %all-to-all-start = ((bf16[32,2,2,64,128]{4,3,2,1,0:T(8,128)(2,1)}), bf16[32,2,2,64,128]{4,3,2,1,0:T(8,128)(2,1)S(1)}, u32[]{:S(2)}, u32[]{:S(2)}) async-start(bf16[32,2,2,64,128]{4,3,2,1,0:T(8,128)(2,1)} %pack.1), calls=%async_computation | async-start | bytes 4194304 | tf_op jit(solution)/shard_map/all_to_all | solution.py:210
  215.6 2.3 copy-start.1
  215.7 4.1 %copy-start = (s32[4096,128]{1,0:T(8,128)S(1)}, s32[4096,128]{1,0:T(8,128)}, u32[]{:S(2)}) copy-start(s32[4096,128]{1,0:T(8,128)} %count_words_0_0.1.words_ref) | copy-start | bytes 6291460
  215.7 6.0 %collective-permute-start = (bf16[32,2,64,128]{3,2,1,0:T(8,128)(2,1)S(1)}, bf16[32,2,64,128]{3,2,1,0:T(8,128)(2,1)S(1)}, u32[]{:S(2)}, u32[]{:S(2)}) collective-permute-start(bf16[32,2,64,128]{3,2,1,0:T(8,128)(2,1)S(1)} %dynamic-slice_bitcast_fusion), channel_id=1, source_target_pairs={{0,16},{16,0},{32,48},{48,32},{64,80},{80,64},{96,112},{112,96},{1... | collective-permute-start | bytes 3145736 | tf_op jit(solution)/shard_map/ppermute | solution.py:222
  219.8 1.9 copy-start.2
  219.8 2.2 copy-start.3
  221.7 18.9 %copy-start.5 = (f32[2,1024]{1,0:T(2,128)S(1)}, f32[2,1024]{1,0:T(2,128)}, u32[]{:S(2)}) copy-start(f32[2,1024]{1,0:T(2,128)} %param.9) | copy-start | bytes 24580
  221.7 19.5 %copy-start.4 = (f32[2,64,1024]{2,1,0:T(8,128)S(1)}, f32[2,64,1024]{2,1,0:T(8,128)}, u32[]{:S(2)}) copy-start(f32[2,64,1024]{2,1,0:T(8,128)} %param.8) | copy-start | bytes 1572868

commit v3 on v2

--- a/solution.py
+++ b/solution.py
@@ -13,45 +13,39 @@
 
 LOW = 128
 DIGITS = 8
-STRIDE = 15
 
 
 def chip_at(place, core, chips):
-    return (STRIDE * (place + core * (chips - 1 - 2 * place))) % chips
-
-
-def place_of(chip, core, chips):
-    place = (pow(STRIDE, -1, chips) * chip) % chips
-    return place + core * (chips - 1 - 2 * place)
+    return (place + core * (chips // 2)) % chips
 
 
 def pack_kernel(core_ref, grads_ref, packed_ref, held, in_done, out_done):
     chips = grads_ref.shape[0]
-    reads = in_done.shape[0]
-    size = chips // reads
+    parts = in_done.shape[0]
+    size = chips // parts
     core = core_ref[0]
 
     def read(i):
+        return pltpu.make_async_copy(
+            grads_ref.at[pl.ds(chip_at(i * size, core, chips), size)],
+            held.at[pl.ds(i * size, size)],
+            in_done.at[i],
+        )
+
+    def write(i):
         part = pl.ds(i * size, size)
-        return pltpu.make_async_copy(grads_ref.at[part], held.at[part], in_done.at[i])
-
-    def write(chip):
-        place = place_of(chip, core, chips)
-        return pltpu.make_async_copy(
-            held.at[chip], packed_ref.at[place], out_done.at[chip]
-        )
-
-    for i in range(reads):
+        return pltpu.make_async_copy(held.at[part], packed_ref.at[part], out_done.at[i])
+
+    for i in range(parts):
         read(i).start()
-    for i in range(reads):
+    for i in range(parts):
         read(i).wait()
-        for chip in range(i * size, (i + 1) * size):
-            write(chip).start()
-    for chip in range(chips):
-        write(chip).wait()
-
-
-def pack(core, grads):
+        write(i).start()
+    for i in range(parts):
+        write(i).wait()
+
+
+def pack(core, grads, parts=8):
     return pl.pallas_call(
         pack_kernel,
         in_specs=[
@@ -62,8 +56,8 @@
         out_shape=jax.ShapeDtypeStruct(grads.shape, grads.dtype),
         scratch_shapes=[
             pltpu.VMEM(grads.shape, grads.dtype),
-            pltpu.SemaphoreType.DMA((4,)),
-            pltpu.SemaphoreType.DMA((grads.shape[0],)),
+            pltpu.SemaphoreType.DMA((parts,)),
+            pltpu.SemaphoreType.DMA((parts,)),
         ],
         cost_estimate=pl.CostEstimate(
             flops=0, bytes_accessed=4 * grads.size, transcendentals=0
@@ -194,6 +188,34 @@
         compiler_params=pltpu.CompilerParams(vmem_limit_bytes=24 << 20),
         name="sibling_half",
     )(arrived, *words, *first)
+
+
+def update_kernel(shared_ref, state_ref, grad_ref, rows_ref, new_rows_ref, new_state_ref):
+    total = shared_ref[0]
+    for copy in range(1, shared_ref.shape[0]):
+        total = total + shared_ref[copy]
+    new_state = state_ref[...] + total / WIDTH
+    new_state_ref[...] = new_state
+    scale = learning_rate / (jnp.sqrt(new_state) + epsilon)
+    for table in range(rows_ref.shape[0]):
+        new_rows_ref[table] = rows_ref[table] - scale[table : table + 1] * grad_ref[table]
+
+
+def update(shared, state, gradient, rows):
+    return pl.pallas_call(
+        update_kernel,
+        in_specs=[pl.BlockSpec(memory_space=pltpu.VMEM)] * 4,
+        out_specs=[pl.BlockSpec(memory_space=pltpu.VMEM)] * 2,
+        out_shape=[
+            jax.ShapeDtypeStruct(rows.shape, jnp.float32),
+            jax.ShapeDtypeStruct(state.shape, jnp.float32),
+        ],
+        cost_estimate=pl.CostEstimate(
+            flops=3 * rows.size, bytes_accessed=12 * rows.size, transcendentals=0
+        ),
+        compiler_params=pltpu.CompilerParams(vmem_limit_bytes=24 << 20),
+        name="update",
+    )(shared, state, gradient, rows)
 
 
 def body(pooled_grad, bag_ids, bag_lengths, table_rows, row_state):
@@ -222,10 +244,8 @@
     swapped = lax.ppermute(other, "tables", [(k, k ^ 1) for k in range(groups)])
     first = [own_half(core, arrived, words[0][table], table) for table in range(members)]
     gradient, squares = sibling_half(swapped, words[1], first, splits)
-    totals = jnp.sum(lax.all_to_all(squares, "cols", 0, 0, tiled=True), axis=0)
-    new_state = row_state + totals / WIDTH
-    scale = learning_rate / (jnp.sqrt(new_state) + epsilon)
-    new_rows = table_rows - scale[:, None, :] * gradient
+    shared = lax.all_to_all(squares, "cols", 0, 0, tiled=True)
+    new_rows, new_state = update(shared, row_state, gradient, table_rows)
     return (new_rows, new_state)
 
 

time: 242 us -> 241 us (level)
  the two profiles are of different devices: /device:TPU:128 before, /device:TPU:256 now
where the time goes in v3:
time: 241 us
  waiting for transfers between devices  170 us (71%)
  starting transfers between devices  27.6 us (11%)
  Pallas kernels  27.3 us (11%)
  blocking collectives  14.8 us (6%)
    all_to_all x1, waiting for transfers between devices, body(): lax.all_to_all(pack(core, grouped), 'tables', 0, 0, tiled=True, axis_inde...  170 us
    all_to_all x1, starting transfers between devices, body(): lax.all_to_all(pack(core, grouped), 'tables', 0, 0, tiled=True, axis_inde...  25.4 us
    pallas_call x4, Pallas kernels, count_words(): pl.pallas_call(functools.partial(words_kernel, chips, owned, table, half)...  16.6 us
    all_to_all x1, blocking collectives, body(): shared = lax.all_to_all(squares, 'cols', 0, 0, tiled=True)  14.8 us
  transfers between devices with their start and end apart: 2, of which 1 were waited for; matrix products, arithmetic and copies ran while one was open for 0% of the time, Pallas kernels for 8%

profile of v3, /device:TPU:256, one launch (start us, length us, event | category | flops | bytes accessed | tf_op | source)
XLA Modules:
  0.0 241.1 jit_solution(8150949415552630877)
XLA Ops:
  0.6 2.4 %pack.1 = bf16[32,2,2,64,128]{4,3,2,1,0:T(8,128)(2,1)} custom-call(s32[1]{0:T(128)} %bitcast.core_ref, bf16[32,2,2,64,128]{4,3,2,1,0:T(8,128)(2,1)} %bitcast.4), custom_call_target="tpu_custom_call" | custom-call | bytes 4194304 | tf_op jit(solution)/shard_map/pack/pallas_call | solution.py:49
  3.1 25.4 %all-to-all-start = ((bf16[32,2,2,64,128]{4,3,2,1,0:T(8,128)(2,1)}), bf16[32,2,2,64,128]{4,3,2,1,0:T(8,128)(2,1)S(1)}, u32[]{:S(2)}, u32[]{:S(2)}) async-start(bf16[32,2,2,64,128]{4,3,2,1,0:T(8,128)(2,1)} %pack.1), calls=%async_computation | async-start | bytes 4194304 | tf_op jit(solution)/shard_map/all_to_all | solution.py:232
  28.5 4.1 %count_words_0_0.1.words_ref = s32[4096,128]{1,0:T(8,128)} custom-call(s32[1]{0:T(128)} %bitcast.core_ref, s32[2,8,8192]{2,1,0:T(8,128)} %ids_ref.7, s32[2,8192]{1,0:T(2,128)} %lens_ref.7), custom_call_target="tpu_custom_call" | custom-call | flops 15000000 | bytes 2500000 | tf_op jit(solution)/shard_map/count_words_0_0/pallas_call | solution.py:92
  32.7 4.2 %count_words_1_0.1.words_ref = s32[4096,128]{1,0:T(8,128)} custom-call(s32[1]{0:T(128)} %bitcast.core_ref, s32[2,8,8192]{2,1,0:T(8,128)} %ids_ref.7, s32[2,8192]{1,0:T(2,128)} %lens_ref.7), custom_call_target="tpu_custom_call" | custom-call | flops 15000000 | bytes 2500000 | tf_op jit(solution)/shard_map/count_words_1_0/pallas_call | solution.py:92
  36.8 4.1 %count_words_0_1.1.refs_1_ = s32[4096,128]{1,0:T(8,128)} custom-call(s32[1]{0:T(128)} %bitcast.core_ref, s32[2,8,8192]{2,1,0:T(8,128)} %ids_ref.7, s32[2,8192]{1,0:T(2,128)} %lens_ref.7), custom_call_target="tpu_custom_call" | custom-call | flops 15000000 | bytes 2500000 | tf_op jit(solution)/shard_map/count_words_0_1/pallas_call | solution.py:92
  40.9 4.2 %count_words_1_1.1.refs_2_ = s32[4096,128]{1,0:T(8,128)} custom-call(s32[1]{0:T(128)} %bitcast.core_ref, s32[2,8,8192]{2,1,0:T(8,128)} %ids_ref.7, s32[2,8192]{1,0:T(2,128)} %lens_ref.7), custom_call_target="tpu_custom_call" | custom-call | flops 15000000 | bytes 2500000 | tf_op jit(solution)/shard_map/count_words_1_1/pallas_call | solution.py:92
  45.1 170.2 %all-to-all-done.arrived_ref = bf16[32,2,2,64,128]{4,3,2,1,0:T(8,128)(2,1)S(1)} async-done(((bf16[32,2,2,64,128]{4,3,2,1,0:T(8,128)(2,1)}), bf16[32,2,2,64,128]{4,3,2,1,0:T(8,128)(2,1)S(1)}, u32[]{:S(2)}, u32[]{:S(2)}) %all-to-all-start) | async-done | bytes 2097184 | tf_op jit(solution)/shard_map/all_to_all | solution.py:232
  215.3 0.0 copy-start.1
  215.3 0.1 dynamic-slice_bitcast_fusion
  215.4 0.0 copy-start
  215.4 2.2 collective-permute-start
  217.6 0.0 copy-done.1
  217.6 1.9 own_half_1.1.refs_4_
  219.5 0.0 copy-done
  219.5 0.0 copy-start.2
  219.5 0.0 copy-start.3
  219.5 1.9 own_half_0.1.refs_3_
  221.4 0.0 copy-start.4
  221.4 0.0 copy-start.5
  221.4 0.0 collective-permute-done.refs_0_
  221.4 0.0 copy-done.2
  221.4 0.3 copy-done.3
  221.7 3.7 %sibling_half.1 = (f32[2,64,1024]{2,1,0:T(8,128)S(1)}, f32[16,2,1024]{2,1,0:T(2,128)S(1)}) custom-call(bf16[32,2,64,128]{3,2,1,0:T(8,128)(2,1)S(1)} %collective-permute-done.refs_0_, s32[4096,128]{1,0:T(8,128)S(1)} %copy-done.2, s32[4096,128]{1,0:T(8,128)S(1)} %copy-done.3, f32[64,1024]{1,0:T(8,128)S(1)} %own_half_0.1.refs_3_, f32[64,1024]{1,0:T(8,128)S(1)} %own_half_1.1.refs_4_), custom_call_target="tpu_custom_call" | custom-call | flops 1073741824 | bytes 6000000 | tf_op jit(solution)/shard_map/sibling_half/pallas_call | solution.py:177
  225.4 14.8 %all_to_all.10.shared_ref = f32[16,2,1024]{2,1,0:T(2,128)S(1)} all-to-all(f32[16,2,1024]{2,1,0:T(2,128)S(1)} %get-tuple-element.14), channel_id=1, replica_groups=mesh['tables'=64,'cols'=16] {'cols'}, dimensions={0} | all-to-all | bytes 262144 | tf_op jit(solution)/shard_map/all_to_all | solution.py:247
  240.2 0.0 copy-done.4
  240.2 0.0 copy-done.5
  240.2 0.9 update.1
Async XLA Ops:
  3.1 212.3 %all-to-all-start = ((bf16[32,2,2,64,128]{4,3,2,1,0:T(8,128)(2,1)}), bf16[32,2,2,64,128]{4,3,2,1,0:T(8,128)(2,1)S(1)}, u32[]{:S(2)}, u32[]{:S(2)}) async-start(bf16[32,2,2,64,128]{4,3,2,1,0:T(8,128)(2,1)} %pack.1), calls=%async_computation | async-start | bytes 4194304 | tf_op jit(solution)/shard_map/all_to_all | solution.py:232
  215.3 2.3 copy-start.1
  215.4 4.1 %copy-start = (s32[4096,128]{1,0:T(8,128)S(1)}, s32[4096,128]{1,0:T(8,128)}, u32[]{:S(2)}) copy-start(s32[4096,128]{1,0:T(8,128)} %count_words_0_0.1.words_ref) | copy-start | bytes 6291460
  215.4 6.0 %collective-permute-start = (bf16[32,2,64,128]{3,2,1,0:T(8,128)(2,1)S(1)}, bf16[32,2,64,128]{3,2,1,0:T(8,128)(2,1)S(1)}, u32[]{:S(2)}, u32[]{:S(2)}) collective-permute-start(bf16[32,2,64,128]{3,2,1,0:T(8,128)(2,1)S(1)} %dynamic-slice_bitcast_fusion), channel_id=1, source_target_pairs={{0,16},{16,0},{32,48},{48,32},{64,80},{80,64},{96,112},{112,96},{1... | collective-permute-start | bytes 3145736 | tf_op jit(solution)/shard_map/ppermute | solution.py:244
  219.5 1.9 copy-start.2
  219.5 2.2 copy-start.3
  221.4 18.9 %copy-start.4 = (f32[2,64,1024]{2,1,0:T(8,128)S(1)}, f32[2,64,1024]{2,1,0:T(8,128)}, u32[]{:S(2)}) copy-start(f32[2,64,1024]{2,1,0:T(8,128)} %rows_ref.1) | copy-start | bytes 1572868
  221.4 18.8 %copy-start.5 = (f32[2,1024]{1,0:T(2,128)S(1)}, f32[2,1024]{1,0:T(2,128)}, u32[]{:S(2)}) copy-start(f32[2,1024]{1,0:T(2,128)} %state_ref.1) | copy-start | bytes 24580

commit v4 on v3

--- a/solution.py
+++ b/solution.py
@@ -66,10 +66,10 @@
     )(core, grads)
 
 
-def words_kernel(chips, owned, table, half, core_ref, ids_ref, lens_ref, words_ref):
+def counts_kernel(chips, owned, table, half, core_ref, ids_ref, lens_ref, counts_ref):
     block = pl.program_id(0)
     source_core = core_ref[0] if half == 0 else 1 - core_ref[0]
-    places = words_ref.shape[0] // owned
+    places = counts_ref.shape[0] // owned
     word = lax.broadcasted_iota(jnp.int32, (LOW, owned), 0)
     for i in range(places):
         chip = chip_at(block * places + i, source_core, chips)
@@ -84,32 +84,54 @@
         total = jnp.zeros((LOW, owned), jnp.int32)
         for k in range(ids.shape[0]):
             total = total + jnp.where(low[k : k + 1] == word, unit[k : k + 1], 0)
-        words_ref[owned * i : owned * (i + 1), :] = total.T
-
-
-def count_words(core, ids, lens, chips, owned, table, half, block=8):
+        words = total.T
+        samples = pl.ds(owned * i, owned)
+        if counts_ref.dtype == jnp.int32:
+            counts_ref[samples, :] = words
+        else:
+            for digit in range(DIGITS):
+                count = lax.shift_right_logical(words, 4 * digit) & 15
+                counts_ref[samples, pl.ds(LOW * digit, LOW)] = count.astype(
+                    jnp.float32
+                ).astype(counts_ref.dtype)
+
+
+def count(core, ids, lens, chips, owned, table, half, packed, block=8):
     tables, positions, samples = ids.shape
+    width, dtype = (LOW, jnp.int32) if packed else (LOW * DIGITS, jnp.float8_e5m2)
     return pl.pallas_call(
-        functools.partial(words_kernel, chips, owned, table, half),
+        functools.partial(counts_kernel, chips, owned, table, half),
         grid=(chips // block,),
         in_specs=[
             pl.BlockSpec(memory_space=pltpu.SMEM),
             pl.BlockSpec((1, positions, samples), lambda i: (table, 0, 0)),
             pl.BlockSpec((tables, samples), lambda i: (0, 0)),
         ],
-        out_specs=pl.BlockSpec((block * owned, LOW), lambda i: (i, 0)),
-        out_shape=jax.ShapeDtypeStruct((chips * owned, LOW), jnp.int32),
+        out_specs=pl.BlockSpec((block * owned, width), lambda i: (i, 0)),
+        out_shape=jax.ShapeDtypeStruct((chips * owned, width), dtype),
         cost_estimate=pl.CostEstimate(
-            flops=15_000_000, bytes_accessed=2_500_000, transcendentals=0
+            flops=15_000_000, bytes_accessed=4_000_000, transcendentals=0
         ),
-        name=f"count_words_{table}_{half}",
+        name=f"count_{table}_{half}",
     )(core, ids, lens)
 
 
-def multiply(arrived, words):
+def part(pair):
+    return slice(2 * LOW * pair, 2 * LOW * (pair + 1))
+
+
+def multiply(arrived, counts_ref):
     grads = jnp.concatenate([arrived[j] for j in range(arrived.shape[0])], axis=1)
     products = []
     for pair in range(DIGITS // 2):
+        if counts_ref.dtype != jnp.int32:
+            products.append(
+                jnp.dot(
+                    grads, counts_ref[:, part(pair)], preferred_element_type=jnp.float32
+                )
+            )
+            continue
+        words = counts_ref[...]
         counts, scales = [], []
         for digit in (2 * pair, 2 * pair + 1):
             top = digit == DIGITS - 1
@@ -127,70 +149,74 @@
     return products
 
 
-def part(pair):
-    return slice(2 * LOW * pair, 2 * LOW * (pair + 1))
-
-
-def own_kernel(table, core_ref, arrived_ref, words_ref, grad_ref):
+def own_kernel(table, core_ref, arrived_ref, counts_ref, grad_ref):
     core = core_ref[0]
     arrived = [arrived_ref[j, core, table] for j in range(arrived_ref.shape[0])]
-    for pair, product in enumerate(multiply(jnp.stack(arrived), words_ref[...])):
+    for pair, product in enumerate(multiply(jnp.stack(arrived), counts_ref)):
         grad_ref[:, part(pair)] = product
 
 
-def own_half(core, arrived, words, table):
+def own_half(core, arrived, counts, table):
     columns = arrived.shape[3]
+    vmem = pl.BlockSpec(memory_space=pltpu.VMEM)
     return pl.pallas_call(
         functools.partial(own_kernel, table),
-        in_specs=[
-            pl.BlockSpec(memory_space=pltpu.SMEM),
-            pl.BlockSpec(memory_space=pltpu.VMEM),
-            pl.BlockSpec(memory_space=pltpu.VMEM),
-        ],
-        out_specs=pl.BlockSpec(memory_space=pltpu.VMEM),
+        in_specs=[pl.BlockSpec(memory_space=pltpu.SMEM), vmem, vmem],
+        out_specs=vmem,
         out_shape=jax.ShapeDtypeStruct((columns, LOW * DIGITS), jnp.float32),
         cost_estimate=pl.CostEstimate(
             flops=536_870_912, bytes_accessed=3_000_000, transcendentals=0
         ),
         compiler_params=pltpu.CompilerParams(vmem_limit_bytes=24 << 20),
         name=f"own_half_{table}",
-    )(core, arrived, words)
-
-
-def sibling_kernel(tables, *refs):
-    arrived_ref = refs[0]
-    words_refs, first_refs = refs[1 : 1 + tables], refs[1 + tables : 1 + 2 * tables]
-    grad_ref, square_ref = refs[1 + 2 * tables :]
+    )(core, arrived, counts)
+
+
+def sibling_kernel(table, arrived_ref, counts_ref, first_ref, *refs):
+    earlier, (grad_ref, square_ref) = refs[:-2], refs[-2:]
+    last = len(square_ref.shape) == 3
+    for pair, product in enumerate(multiply(arrived_ref[:, table], counts_ref)):
+        product = product + first_ref[:, part(pair)]
+        grad_ref[:, part(pair)] = product
+        square = jnp.sum(product * product, axis=0, keepdims=True)
+        if not last:
+            square_ref[:, part(pair)] = square
+            continue
+        squares = [ref[:, part(pair)] for ref in earlier] + [square]
+        for copy in range(square_ref.shape[0]):
+            for row, value in enumerate(squares):
+                square_ref[copy, row : row + 1, part(pair)] = value
+
+
+def sibling_half(arrived, counts, first, copies):
+    tables, columns = arrived.shape[1:3]
+    rows = LOW * DIGITS
+    vmem = pl.BlockSpec(memory_space=pltpu.VMEM)
+    gradients, squares = [], []
     for table in range(tables):
-        products = multiply(arrived_ref[:, table], words_refs[table][...])
-        for pair, product in enumerate(products):
-            product = product + first_refs[table][:, part(pair)]
-            grad_ref[table, :, part(pair)] = product
-            square = jnp.sum(product * product, axis=0, keepdims=True)
-            for copy in range(square_ref.shape[0]):
-                square_ref[copy, table : table + 1, part(pair)] = square
-
-
-def sibling_half(arrived, words, first, copies):
-    _, tables, columns, _ = arrived.shape
-    rows = LOW * DIGITS
-    return pl.pallas_call(
-        functools.partial(sibling_kernel, tables),
-        in_specs=[pl.BlockSpec(memory_space=pltpu.VMEM)] * (1 + 2 * tables),
-        out_specs=[pl.BlockSpec(memory_space=pltpu.VMEM)] * 2,
-        out_shape=[
-            jax.ShapeDtypeStruct((tables, columns, rows), jnp.float32),
-            jax.ShapeDtypeStruct((copies, tables, rows), jnp.float32),
-        ],
-        cost_estimate=pl.CostEstimate(
-            flops=1_073_741_824, bytes_accessed=6_000_000, transcendentals=0
-        ),
-        compiler_params=pltpu.CompilerParams(vmem_limit_bytes=24 << 20),
-        name="sibling_half",
-    )(arrived, *words, *first)
-
-
-def update_kernel(shared_ref, state_ref, grad_ref, rows_ref, new_rows_ref, new_state_ref):
+        earlier = squares if table == tables - 1 else []
+        shape = (copies, tables, rows) if table == tables - 1 else (1, rows)
+        gradient, square = pl.pallas_call(
+            functools.partial(sibling_kernel, table),
+            in_specs=[vmem] * (3 + len(earlier)),
+            out_specs=[vmem] * 2,
+            out_shape=[
+                jax.ShapeDtypeStruct((columns, rows), jnp.float32),
+                jax.ShapeDtypeStruct(shape, jnp.float32),
+            ],
+            cost_estimate=pl.CostEstimate(
+                flops=536_870_912, bytes_accessed=5_000_000, transcendentals=0
+            ),
+            compiler_params=pltpu.CompilerParams(vmem_limit_bytes=24 << 20),
+            name=f"sibling_half_{table}",
+        )(arrived, counts[table], first[table], *earlier)
+        gradients.append(gradient)
+        squares = squares + [square]
+    return gradients, squares[-1]
+
+
+def update_kernel(shared_ref, state_ref, rows_ref, *refs):
+    grad_refs, (new_rows_ref, new_state_ref) = refs[:-2], refs[-2:]
     total = shared_ref[0]
     for copy in range(1, shared_ref.shape[0]):
         total = total + shared_ref[copy]
@@ -198,13 +224,14 @@
     new_state_ref[...] = new_state
     scale = learning_rate / (jnp.sqrt(new_state) + epsilon)
     for table in range(rows_ref.shape[0]):
-        new_rows_ref[table] = rows_ref[table] - scale[table : table + 1] * grad_ref[table]
-
-
-def update(shared, state, gradient, rows):
+        step = scale[table : table + 1] * grad_refs[table][...]
+        new_rows_ref[table] = rows_ref[table] - step
+
+
+def update(shared, state, rows, gradients):
     return pl.pallas_call(
         update_kernel,
-        in_specs=[pl.BlockSpec(memory_space=pltpu.VMEM)] * 4,
+        in_specs=[pl.BlockSpec(memory_space=pltpu.VMEM)] * (3 + len(gradients)),
         out_specs=[pl.BlockSpec(memory_space=pltpu.VMEM)] * 2,
         out_shape=[
             jax.ShapeDtypeStruct(rows.shape, jnp.float32),
@@ -215,7 +242,7 @@
         ),
         compiler_params=pltpu.CompilerParams(vmem_limit_bytes=24 << 20),
         name="update",
-    )(shared, state, gradient, rows)
+    )(shared, state, rows, *gradients)
 
 
 def body(pooled_grad, bag_ids, bag_lengths, table_rows, row_state):
@@ -232,20 +259,31 @@
     arrived = lax.all_to_all(
         pack(core, grouped), "tables", 0, 0, tiled=True, axis_index_groups=orders
     )
-    words = [
+    counts = [
         [
-            count_words(core, bag_ids, bag_lengths, chips, owned, table, half)
+            count(
+                core,
+                bag_ids,
+                bag_lengths,
+                chips,
+                owned,
+                table,
+                half,
+                packed=half == 0 or table < members - 1,
+            )
             for table in range(members)
         ]
         for half in range(2)
     ]
-    arrived, words = lax.optimization_barrier((arrived, words))
+    arrived, counts = lax.optimization_barrier((arrived, counts))
     other = lax.dynamic_index_in_dim(arrived, 1 - core[0], 1, keepdims=False)
     swapped = lax.ppermute(other, "tables", [(k, k ^ 1) for k in range(groups)])
-    first = [own_half(core, arrived, words[0][table], table) for table in range(members)]
-    gradient, squares = sibling_half(swapped, words[1], first, splits)
+    first = [
+        own_half(core, arrived, counts[0][table], table) for table in range(members)
+    ]
+    gradients, squares = sibling_half(swapped, counts[1], first, splits)
     shared = lax.all_to_all(squares, "cols", 0, 0, tiled=True)
-    new_rows, new_state = update(shared, row_state, gradient, table_rows)
+    new_rows, new_state = update(shared, row_state, table_rows, gradients)
     return (new_rows, new_state)
 
 

time: 241 us -> 240 us (level)
    pallas_call x5 -> x6, Pallas kernels: 20.3 us -> 21 us  [the longest x4 18.4 us: count(): pl.pallas_call(functools.partial(counts_kernel, chips, owned, table, half...]
  transfers between devices with their start and end apart: 2 -> 2, of which waited for: 1 -> 1; matrix products, arithmetic and copies ran while one was open for 0% -> 0% of each run, Pallas kernels for 8% -> 9%
where the time goes in v4:
time: 240 us
  waiting for transfers between devices  168 us (70%)
  Pallas kernels  28.1 us (12%)
  starting transfers between devices  27.6 us (12%)
  blocking collectives  14.8 us (6%)
    all_to_all x1, waiting for transfers between devices, body(): lax.all_to_all(pack(core, grouped), 'tables', 0, 0, tiled=True, axis_inde...  168 us
    all_to_all x1, starting transfers between devices, body(): lax.all_to_all(pack(core, grouped), 'tables', 0, 0, tiled=True, axis_inde...  25.4 us
    pallas_call x4, Pallas kernels, count(): pl.pallas_call(functools.partial(counts_kernel, chips, owned, table, half...  18.4 us
    all_to_all x1, blocking collectives, body(): shared = lax.all_to_all(squares, 'cols', 0, 0, tiled=True)  14.8 us
  transfers between devices with their start and end apart: 2, of which 1 were waited for; matrix products, arithmetic and copies ran while one was open for 0% of the time, Pallas kernels for 9%

profile of v4, /device:TPU:256, one launch (start us, length us, event | category | flops | bytes accessed | tf_op | source)
XLA Modules:
  0.0 239.8 jit_solution(8054285997848611920)
XLA Ops:
  0.6 2.4 %pack.1 = bf16[32,2,2,64,128]{4,3,2,1,0:T(8,128)(2,1)} custom-call(s32[1]{0:T(128)} %bitcast.core_ref, bf16[32,2,2,64,128]{4,3,2,1,0:T(8,128)(2,1)} %bitcast.4), custom_call_target="tpu_custom_call" | custom-call | bytes 4194304 | tf_op jit(solution)/shard_map/pack/pallas_call | solution.py:49
  3.1 25.4 %all-to-all-start = ((bf16[32,2,2,64,128]{4,3,2,1,0:T(8,128)(2,1)}), bf16[32,2,2,64,128]{4,3,2,1,0:T(8,128)(2,1)S(1)}, u32[]{:S(2)}, u32[]{:S(2)}) async-start(bf16[32,2,2,64,128]{4,3,2,1,0:T(8,128)(2,1)} %pack.1), calls=%async_computation | async-start | bytes 4194304 | tf_op jit(solution)/shard_map/all_to_all | solution.py:259
  28.5 4.2 %count_1_0.1.counts_ref = s32[4096,128]{1,0:T(8,128)} custom-call(s32[1]{0:T(128)} %bitcast.core_ref, s32[2,8,8192]{2,1,0:T(8,128)} %ids_ref.7, s32[2,8192]{1,0:T(2,128)} %lens_ref.7), custom_call_target="tpu_custom_call" | custom-call | flops 15000000 | bytes 4000000 | tf_op jit(solution)/shard_map/count_1_0/pallas_call | solution.py:102
  32.8 4.1 %count_0_0.1.counts_ref = s32[4096,128]{1,0:T(8,128)} custom-call(s32[1]{0:T(128)} %bitcast.core_ref, s32[2,8,8192]{2,1,0:T(8,128)} %ids_ref.7, s32[2,8192]{1,0:T(2,128)} %lens_ref.7), custom_call_target="tpu_custom_call" | custom-call | flops 15000000 | bytes 4000000 | tf_op jit(solution)/shard_map/count_0_0/pallas_call | solution.py:102
  36.9 4.2 %count_0_1.1.counts_ref = s32[4096,128]{1,0:T(8,128)} custom-call(s32[1]{0:T(128)} %bitcast.core_ref, s32[2,8,8192]{2,1,0:T(8,128)} %ids_ref.7, s32[2,8192]{1,0:T(2,128)} %lens_ref.7), custom_call_target="tpu_custom_call" | custom-call | flops 15000000 | bytes 4000000 | tf_op jit(solution)/shard_map/count_0_1/pallas_call | solution.py:102
  41.1 5.9 %count_1_1.1.counts_ref = f8e5m2[4096,1024]{1,0:T(32,128)(4,1)} custom-call(s32[1]{0:T(128)} %bitcast.core_ref, s32[2,8,8192]{2,1,0:T(8,128)} %ids_ref.7, s32[2,8192]{1,0:T(2,128)} %lens_ref.7), custom_call_target="tpu_custom_call" | custom-call | flops 15000000 | bytes 4000000 | tf_op jit(solution)/shard_map/count_1_1/pallas_call | solution.py:102
  47.0 168.4 %all-to-all-done.arrived_ref = bf16[32,2,2,64,128]{4,3,2,1,0:T(8,128)(2,1)S(1)} async-done(((bf16[32,2,2,64,128]{4,3,2,1,0:T(8,128)(2,1)}), bf16[32,2,2,64,128]{4,3,2,1,0:T(8,128)(2,1)S(1)}, u32[]{:S(2)}, u32[]{:S(2)}) %all-to-all-start) | async-done | bytes 2097184 | tf_op jit(solution)/shard_map/all_to_all | solution.py:259
  215.3 0.0 copy-start.3
  215.3 0.1 dynamic-slice_bitcast_fusion
  215.4 0.0 copy-start.2
  215.4 2.2 collective-permute-start
  217.6 0.0 copy-done.3
  217.6 0.0 copy-start.1
  217.6 1.9 own_half_1.1.first_ref
  219.5 0.0 copy-done.2
  219.5 0.0 copy-start
  219.5 1.9 own_half_0.1.first_ref
  221.4 0.0 collective-permute-done.arrived_ref
  221.4 0.0 copy-done.1
  221.4 1.9 sibling_half_0.1
  223.3 0.0 copy-done
  223.3 0.0 copy-start.4
  223.3 0.0 copy-start.5
  223.3 0.7 sibling_half_1.1
  224.1 14.8 %all_to_all.10.shared_ref = f32[16,2,1024]{2,1,0:T(2,128)S(1)} all-to-all(f32[16,2,1024]{2,1,0:T(2,128)S(1)} %get-tuple-element.17), channel_id=1, replica_groups=mesh['tables'=64,'cols'=16] {'cols'}, dimensions={0} | all-to-all | bytes 262144 | tf_op jit(solution)/shard_map/all_to_all | solution.py:285
  238.9 0.0 copy-done.4
  238.9 0.0 copy-done.5
  238.9 0.9 update.1
Async XLA Ops:
  3.1 212.3 %all-to-all-start = ((bf16[32,2,2,64,128]{4,3,2,1,0:T(8,128)(2,1)}), bf16[32,2,2,64,128]{4,3,2,1,0:T(8,128)(2,1)S(1)}, u32[]{:S(2)}, u32[]{:S(2)}) async-start(bf16[32,2,2,64,128]{4,3,2,1,0:T(8,128)(2,1)} %pack.1), calls=%async_computation | async-start | bytes 4194304 | tf_op jit(solution)/shard_map/all_to_all | solution.py:259
  215.3 2.3 copy-start.3
  215.4 4.1 %copy-start.2 = (s32[4096,128]{1,0:T(8,128)S(1)}, s32[4096,128]{1,0:T(8,128)}, u32[]{:S(2)}) copy-start(s32[4096,128]{1,0:T(8,128)} %count_0_0.1.counts_ref) | copy-start | bytes 6291460
  215.4 5.9 %collective-permute-start = (bf16[32,2,64,128]{3,2,1,0:T(8,128)(2,1)S(1)}, bf16[32,2,64,128]{3,2,1,0:T(8,128)(2,1)S(1)}, u32[]{:S(2)}, u32[]{:S(2)}) collective-permute-start(bf16[32,2,64,128]{3,2,1,0:T(8,128)(2,1)S(1)} %dynamic-slice_bitcast_fusion), channel_id=1, source_target_pairs={{0,16},{16,0},{32,48},{48,32},{64,80},{80,64},{96,112},{112,96},{1... | collective-permute-start | bytes 3145736 | tf_op jit(solution)/shard_map/ppermute | solution.py:280
  217.6 3.8 %copy-start.1 = (s32[4096,128]{1,0:T(8,128)S(1)}, s32[4096,128]{1,0:T(8,128)}, u32[]{:S(2)}) copy-start(s32[4096,128]{1,0:T(8,128)} %count_0_1.1.counts_ref) | copy-start | bytes 6291460
  219.5 3.8 %copy-start = (f8e5m2[4096,1024]{1,0:T(32,128)(4,1)S(1)}, f8e5m2[4096,1024]{1,0:T(32,128)(4,1)}, u32[]{:S(2)}) copy-start(f8e5m2[4096,1024]{1,0:T(32,128)(4,1)} %count_1_1.1.counts_ref) | copy-start | bytes 12582916
  223.3 15.6 %copy-start.4 = (f32[2,64,1024]{2,1,0:T(8,128)S(1)}, f32[2,64,1024]{2,1,0:T(8,128)}, u32[]{:S(2)}) copy-start(f32[2,64,1024]{2,1,0:T(8,128)} %rows_ref.1) | copy-start | bytes 1572868
  223.3 15.6 %copy-start.5 = (f32[2,1024]{1,0:T(2,128)S(1)}, f32[2,1024]{1,0:T(2,128)}, u32[]{:S(2)}) copy-start(f32[2,1024]{1,0:T(2,128)} %state_ref.1) | copy-start | bytes 24580
